TPU v7x, 32 devices: a whole 2x2x4 slice. The times are simulated.
32 devices in a mesh: tm: 16 (over z, y, x), tile: 2 (over core).
Axes of the slice: x: 2, y: 2, z: 4, core: 2. Of those that a mesh axis runs over, the one named last changes fastest.
Arguments:
- pivot_inverse: bfloat16 [16, 1024, 1024], P('tm', 'tile'), may hold values from -0.2 to 8.2, as said below
- mult_left: bfloat16 [16, 1024, 1024], P('tm', 'tile'), may hold values from -0.09375 to 0.09375
- mult_right: bfloat16 [16, 1024, 1024], P('tm', 'tile'), may hold values from -0.09375 to 0.09375
- mult_tip: bfloat16 [16, 64, 1024], P('tm', 'tile'), may hold values from -0.09375 to 0.09375
- root_cross: bfloat16 [64, 1024], P(None, 'tile'), may hold values from -0.59765625 to 0.59765625
- root_tip: bfloat16 [64, 64], replicated, may hold values from -0.2 to 8.2, as said below
Outputs:
- marginal_cov: bfloat16 [16, 1024, 1024], P('tm', 'tile')
- cross_cov: bfloat16 [16, 1024, 2048], P('tm', 'tile')
- tip_cov: bfloat16 [16, 64, 1024], P('tm', None, 'tile')
Inputs may be any that keep to these rules, and one draw needn't show every extreme that they name: `pivot_inverse`: each of the 16 matrices is symmetric. `root_tip`: symmetric.
All inputs are finite; a program needn't handle non-finite values.
Results may differ from a plain program's by a relative error of at most 0.006.
Values may be sent and summed in bfloat16 or wider, within the bound.
A program may use at most 128 MiB of HBM per device.

v0:
```python
import jax
import jax.numpy as jnp
from jax import lax
from jax.sharding import PartitionSpec as P


def from_behind(shard, axis, by):
    devices = lax.axis_size(axis)
    return lax.ppermute(shard, axis, [(i, (i + by) % devices) for i in range(devices)])


def product(left_matrix, right_matrix):
    return jnp.dot(left_matrix, right_matrix, preferred_element_type=jnp.float32)


def pivot_test(block, level_index):
    return jnp.mod(block, 2 ** (level_index + 1)) == 2**level_index - 1


def body(pivot_inverse, mult_left, mult_right, mult_tip, root_cross, root_tip):
    part_count = lax.axis_size("tm")
    level_count = part_count.bit_length() - 1
    block = jnp.mod(lax.axis_index("tm") + 5, part_count)
    tile_index = lax.axis_index("tile")
    tile_rows = pivot_inverse.shape[1]
    own_start = tile_index * tile_rows
    own_left = mult_left[0]
    own_right = mult_right[0]
    inverse_rows = pivot_inverse[0]
    full_left, full_right, full_tip = (
        lax.all_gather(own_left, "tile", axis=0, tiled=True),
        lax.all_gather(own_right, "tile", axis=0, tiled=True),
        lax.all_gather(mult_tip[0], "tile", axis=0, tiled=True),
    )
    stacked = jnp.concatenate([full_left, full_right, full_tip], axis=0)
    is_root = block == part_count - 1
    tip_cols = lax.dynamic_slice_in_dim(full_tip, own_start, tile_rows, 1)
    zero_rows = jnp.zeros_like(inverse_rows)
    zero_tip = jnp.zeros_like(root_cross)
    diag_rows = jnp.where(is_root, inverse_rows, zero_rows)
    tip_block = jnp.where(is_root, root_cross, zero_tip)
    self_left = zero_rows
    self_right = zero_rows
    near_left = zero_rows
    near_right = zero_rows
    tip_own = product(root_tip, tip_cols)
    for level_index in reversed(range(level_count)):
        distance = 2**level_index
        active = pivot_test(block, level_index)
        has_left = block >= distance
        left_lower = jnp.mod(block - distance, 2 ** (level_index + 2)) == 2 ** (level_index + 1) - 1
        left_diag, left_tip, left_self = from_behind(
            (diag_rows, tip_block, self_right), "tm", distance
        )
        right_diag, right_tip, right_near = from_behind(
            (diag_rows, tip_block, near_left), "tm", -distance
        )
        left_right = jnp.where(left_lower, left_self, right_near)
        left_right = jnp.where(has_left, left_right, zero_rows)
        right_left = lax.all_to_all(left_right, "tile", split_axis=1, concat_axis=0, tiled=True).T
        left_diag = jnp.where(has_left, left_diag, zero_rows)
        left_tip = jnp.where(has_left, left_tip, zero_tip)
        left_right = jnp.where(has_left, left_right, zero_rows)
        right_left = jnp.where(has_left, right_left, zero_rows)
        operand = jnp.concatenate(
            [
                jnp.concatenate([left_diag, left_right, left_tip.T], axis=1),
                jnp.concatenate([right_left, right_diag, right_tip.T], axis=1),
            ],
            axis=0,
        )
        fresh_both = (-product(operand, stacked)).astype(jnp.bfloat16)
        fresh_a = fresh_both[:tile_rows]
        fresh_b = fresh_both[tile_rows:]
        tip_part = product(left_tip, own_left) + product(right_tip, own_right)
        tip_sum = lax.psum_scatter(tip_part, "tile", scatter_dimension=1, tiled=True)
        fresh_tip = (-(tip_sum + tip_own)).astype(jnp.bfloat16)
        turned = lax.all_to_all(
            jnp.stack([fresh_a, fresh_b]), "tile", split_axis=2, concat_axis=1, tiled=True
        )
        own_a = turned[0].T
        own_b = turned[1].T
        total = product(jnp.concatenate([own_a, own_b, fresh_tip.T], axis=1), stacked)
        fresh_diag = (inverse_rows.astype(jnp.float32) - total).astype(jnp.bfloat16)
        diag_rows = jnp.where(active, fresh_diag, diag_rows)
        tip_block = jnp.where(active, fresh_tip, tip_block)
        near_left = jnp.where(active, fresh_a, near_left)
        near_right = jnp.where(active, fresh_b, near_right)
        self_left = jnp.where(active, own_a, self_left)
        self_right = jnp.where(active, own_b, self_right)
    crossing = jnp.concatenate([self_left, self_right], axis=1)
    return (diag_rows[None], crossing[None], tip_block[None])


def solution(mesh):
    placed = (
        P("tm", "tile", None),
        P("tm", "tile", None),
        P("tm", "tile", None),
        P("tm", "tile", None),
        P(None, "tile"),
        P(),
    )
    return jax.shard_map(
        body,
        mesh=mesh,
        in_specs=placed,
        out_specs=(P("tm", "tile", None), P("tm", "tile", None), P("tm", None, "tile")),
        check_vma=False,
    )
```

profile of v0, /device:TPU:0, one launch (start us, length us, event | category | flops | bytes accessed | tf_op | source)
XLA Modules:
  0.0 550.8 jit_solution(8927440939641606121)
XLA Ops:
  7.3 4.1 collective-permute-start.2
  21.1 6.7 %reduce-scatter.5.cloned.1.call-done = f32[64,512]{1,0:T(8,128)} async-done(((f32[64,1024]{1,0:T(8,128)}), f32[64,512]{1,0:T(8,128)}) %reduce-scatter.5.cloned.1.call-update) | async-done | bytes 131088 | tf_op jit(solution)/shard_map/reduce_scatter | solution.py:76
  50.9 60.3 %collective-permute-done.1 = bf16[512,1024]{1,0:T(8,128)(2,1)S(1)} collective-permute-done((bf16[512,1024]{1,0:T(8,128)(2,1)}, bf16[512,1024]{1,0:T(8,128)(2,1)S(1)}, u32[]{:S(2)}, u32[]{:S(2)}) %collective-permute-start.1) | collective-permute-done | bytes 1048608 | tf_op jit(solution)/shard_map/ppermute | solution.py:9
  112.4 4.7 all_to_all.112
  121.2 12.5 %collective-permute-done = bf16[512,1024]{1,0:T(8,128)(2,1)S(1)} collective-permute-done((bf16[512,1024]{1,0:T(8,128)(2,1)}, bf16[512,1024]{1,0:T(8,128)(2,1)S(1)}, u32[]{:S(2)}, u32[]{:S(2)}) %collective-permute-start) | collective-permute-done | bytes 1048608 | tf_op jit(solution)/shard_map/ppermute | solution.py:9
  145.4 8.3 %negate_convert_fusion.3 = bf16[1024,1024]{1,0:T(8,128)(2,1)S(1)} fusion(bf16[512,64]{1,0:T(8,128)(2,1)} %copy.59, bf16[512,1024]{1,0:T(8,128)(2,1)S(1)} %copy-done.19, bf16[512,1024]{1,0:T(8,128)(2,1)} %bitcast.238, bf16[512,64]{1,0:T(8,128)(2,1)} %copy.56, bf16[512,1024]{1,0:T(8,128)(2,1)} %get-tuple-element.42, ...), kind=kOutput, calls=%fused_computation.52 | convolution fusion | flops 4470210560 | bytes 10747904 | tf_op jit(solution)/shard_map/dot_general | solution.py:13
  156.3 6.2 %copy.60 = bf16[2,512,1024]{1,0,2:T(2,128)(2,1)} copy(bf16[2,512,1024]{2,1,0:T(8,128)(2,1)} %pad_maximum_fusion.1) | data formatting | bytes 4194304 | tf_op jit(solution)/shard_map/stack | solution.py:79
  162.5 6.6 %all_to_all.113 = bf16[2,512,1024]{1,0,2:T(2,128)(2,1)S(1)} all-to-all(bf16[2,512,1024]{1,0,2:T(2,128)(2,1)} %copy.60), channel_id=1, replica_groups=mesh['tm'=16,'tile'=2] {'tile'}, dimensions={2} | all-to-all | bytes 4194304 | tf_op jit(solution)/shard_map/all_to_all | solution.py:78
  174.1 4.3 collective-permute-start.5
  191.9 10.4 %collective-permute-done.4 = bf16[512,1024]{1,0:T(8,128)(2,1)} collective-permute-done((bf16[512,1024]{1,0:T(8,128)(2,1)}, bf16[512,1024]{1,0:T(8,128)(2,1)}, u32[]{:S(2)}, u32[]{:S(2)}) %collective-permute-start.4) | collective-permute-done | bytes 1048608 | tf_op jit(solution)/shard_map/ppermute | solution.py:9
  202.3 21.1 %collective-permute-start.20 = (bf16[64,512]{1,0:T(8,128)(2,1)S(1)}, bf16[64,512]{1,0:T(8,128)(2,1)}, u32[]{:S(2)}, u32[]{:S(2)}) collective-permute-start(bf16[64,512]{1,0:T(8,128)(2,1)S(1)} %get-tuple-element.13), channel_id=1, source_target_pairs={{0,30},{2,0},{4,2},{6,4},{8,6},{10,8},{12,10},{14,12},{16,14},{18,... | collective-permute-start | bytes 196616 | tf_op jit(solution)/shard_map/ppermute | solution.py:9
  226.0 4.6 all_to_all.114
  233.9 13.4 %collective-permute-done.3 = bf16[512,1024]{1,0:T(8,128)(2,1)} collective-permute-done((bf16[512,1024]{1,0:T(8,128)(2,1)}, bf16[512,1024]{1,0:T(8,128)(2,1)}, u32[]{:S(2)}, u32[]{:S(2)}) %collective-permute-start.3) | collective-permute-done | bytes 1048608 | tf_op jit(solution)/shard_map/ppermute | solution.py:9
  248.6 19.6 %collective-permute-done.7 = bf16[512,1024]{1,0:T(8,128)(2,1)} collective-permute-done((bf16[512,1024]{1,0:T(8,128)(2,1)}, bf16[512,1024]{1,0:T(8,128)(2,1)}, u32[]{:S(2)}, u32[]{:S(2)}) %collective-permute-start.7) | collective-permute-done | bytes 1048608 | tf_op jit(solution)/shard_map/ppermute | solution.py:9
  268.2 7.7 %negate_convert_fusion.2 = bf16[1024,1024]{1,0:T(8,128)(2,1)S(1)} fusion(bf16[512,64]{1,0:T(8,128)(2,1)} %copy.66, bf16[512,1024]{1,0:T(8,128)(2,1)} %collective-permute-done.7, bf16[512,1024]{1,0:T(8,128)(2,1)S(1)} %bitcast.239, bf16[512,64]{1,0:T(8,128)(2,1)} %copy.63, bf16[512,1024]{1,0:T(8,128)(2,1)S(1)} %copy-done.12, ...), kind=kOutput, calls=%fused_computation.51 | convolution fusion | flops 4470210560 | bytes 10747904 | tf_op jit(solution)/shard_map/dot_general | solution.py:13
  279.8 6.2 %copy.67 = bf16[2,512,1024]{1,0,2:T(2,128)(2,1)} copy(bf16[2,512,1024]{2,1,0:T(8,128)(2,1)} %pad_maximum_fusion.2) | data formatting | bytes 4194304 | tf_op jit(solution)/shard_map/stack | solution.py:79
  286.0 6.6 %all_to_all.115 = bf16[2,512,1024]{1,0,2:T(2,128)(2,1)S(1)} all-to-all(bf16[2,512,1024]{1,0,2:T(2,128)(2,1)} %copy.67), channel_id=1, replica_groups=mesh['tm'=16,'tile'=2] {'tile'}, dimensions={2} | all-to-all | bytes 4194304 | tf_op jit(solution)/shard_map/all_to_all | solution.py:78
  297.6 4.9 collective-permute-start.11
  302.8 5.0 fusion.101
  308.9 4.8 collective-permute-start.13
  314.8 51.6 %collective-permute-done.10 = bf16[512,1024]{1,0:T(8,128)(2,1)} collective-permute-done((bf16[512,1024]{1,0:T(8,128)(2,1)}, bf16[512,1024]{1,0:T(8,128)(2,1)}, u32[]{:S(2)}, u32[]{:S(2)}) %collective-permute-start.10) | collective-permute-done | bytes 1048608 | tf_op jit(solution)/shard_map/ppermute | solution.py:9
  370.5 4.6 all_to_all.116
  376.5 11.9 %collective-permute-done.9 = bf16[512,1024]{1,0:T(8,128)(2,1)} collective-permute-done((bf16[512,1024]{1,0:T(8,128)(2,1)}, bf16[512,1024]{1,0:T(8,128)(2,1)}, u32[]{:S(2)}, u32[]{:S(2)}) %collective-permute-start.9) | collective-permute-done | bytes 1048608 | tf_op jit(solution)/shard_map/ppermute | solution.py:9
  390.7 7.6 %negate_convert_fusion.1 = bf16[1024,1024]{1,0:T(8,128)(2,1)S(1)} fusion(bf16[512,64]{1,0:T(8,128)(2,1)S(1)} %copy-done.31, bf16[512,1024]{1,0:T(8,128)(2,1)} %collective-permute-done.13, bf16[512,1024]{1,0:T(8,128)(2,1)S(1)} %bitcast.240, bf16[512,64]{1,0:T(8,128)(2,1)S(1)} %copy-done.30, bf16[512,1024]{1,0:T(8,128)(2,1)S(1)} %get-tuple-element.15, ...), kind=kOutput, calls=%fused_computation.50 | convolution fusion | flops 4470210560 | bytes 10747904 | tf_op jit(solution)/shard_map/dot_general | solution.py:13
  403.8 6.6 %all_to_all.117 = bf16[2,512,1024]{1,0,2:T(2,128)(2,1)S(1)} all-to-all(bf16[2,512,1024]{1,0,2:T(2,128)(2,1)} %copy.74), channel_id=1, replica_groups=mesh['tm'=16,'tile'=2] {'tile'}, dimensions={2} | all-to-all | bytes 4194304 | tf_op jit(solution)/shard_map/all_to_all | solution.py:78
  428.3 4.2 collective-permute-start.19
  434.1 52.2 %collective-permute-done.16 = bf16[512,1024]{1,0:T(8,128)(2,1)} collective-permute-done((bf16[512,1024]{1,0:T(8,128)(2,1)S(1)}, bf16[512,1024]{1,0:T(8,128)(2,1)}, u32[]{:S(2)}, u32[]{:S(2)}) %collective-permute-start.16) | collective-permute-done | bytes 1048608 | tf_op jit(solution)/shard_map/ppermute | solution.py:9
  487.8 4.6 all_to_all.118
  493.8 14.3 %collective-permute-done.15 = bf16[512,1024]{1,0:T(8,128)(2,1)} collective-permute-done((bf16[512,1024]{1,0:T(8,128)(2,1)}, bf16[512,1024]{1,0:T(8,128)(2,1)}, u32[]{:S(2)}, u32[]{:S(2)}) %collective-permute-start.15) | collective-permute-done | bytes 1048608 | tf_op jit(solution)/shard_map/ppermute | solution.py:9
  510.7 7.6 %negate_convert_fusion = bf16[1024,1024]{1,0:T(8,128)(2,1)S(1)} fusion(bf16[512,64]{1,0:T(8,128)(2,1)S(1)} %copy-done.34, bf16[512,1024]{1,0:T(8,128)(2,1)} %collective-permute-done.19, bf16[512,1024]{1,0:T(8,128)(2,1)S(1)} %bitcast.241, bf16[512,64]{1,0:T(8,128)(2,1)S(1)} %copy-done.33, bf16[512,1024]{1,0:T(8,128)(2,1)S(1)} %get-tuple-element.11, ...), kind=kOutput, calls=%fused_computation.49 | convolution fusion | flops 4470210560 | bytes 10747904 | tf_op jit(solution)/shard_map/dot_general | solution.py:13
  522.8 6.9 %all_to_all.119 = bf16[2,512,1024]{1,0,2:T(2,128)(2,1)S(1)} all-to-all(bf16[2,512,1024]{1,0,2:T(2,128)(2,1)} %copy.81), channel_id=1, replica_groups=mesh['tm'=16,'tile'=2] {'tile'}, dimensions={2} | all-to-all | bytes 4194304 | tf_op jit(solution)/shard_map/all_to_all | solution.py:78
  538.5 4.9 fusion.95
  (218 shorter events, 140.5 us)
Async XLA Ops:
  7.2 20.6 %copy-start.23 = (bf16[64,512]{1,0:T(8,128)(2,1)S(1)}, bf16[64,512]{1,0:T(8,128)(2,1)}, u32[]{:S(2)}) copy-start(bf16[64,512]{1,0:T(8,128)(2,1)} %param.10) | copy-start | bytes 196612
  7.2 20.6 %reduce-scatter.5.cloned.1.call-start = ((), (), s32[]{:S(2)}) async-start(), calls=%async_computation.12 | async-start | bytes 393216 | tf_op jit(solution)/shard_map/reduce_scatter | solution.py:76
  7.3 27.5 %copy-start.2 = (bf16[1,512,1024]{2,1,0:T(8,128)(2,1)S(1)}, bf16[1,512,1024]{2,1,0:T(8,128)(2,1)}, u32[]{:S(2)}) copy-start(bf16[1,512,1024]{2,1,0:T(8,128)(2,1)} %param.8) | copy-start | bytes 3145732
  7.3 7.8 %collective-permute-start.2 = (bf16[64,512]{1,0:T(8,128)(2,1)S(1)}, bf16[64,512]{1,0:T(8,128)(2,1)S(1)}, u32[]{:S(2)}, u32[]{:S(2)}) collective-permute-start(bf16[64,512]{1,0:T(8,128)(2,1)S(1)} %broadcast_select_fusion.26), channel_id=1, source_target_pairs={{0,16},{2,18},{4,20},{6,22},{8,24},{10,26},{12,28},{14,30},{16,0},... | collective-permute-start | bytes 196616 | tf_op jit(solution)/shard_map/ppermute | solution.py:9
  16.6 21.9 %copy-start.4 = (bf16[1,512,1024]{2,1,0:T(8,128)(2,1)S(1)}, bf16[1,512,1024]{2,1,0:T(8,128)(2,1)}, u32[]{:S(2)}) copy-start(bf16[1,512,1024]{2,1,0:T(8,128)(2,1)} %param.7) | copy-start | bytes 3145732
  18.9 98.2 %reduce-scatter.7.cloned.1.call-start = ((), (), s32[]{:S(2)}) async-start(), calls=%async_computation.13 | async-start | bytes 393216 | tf_op jit(solution)/shard_map/reduce_scatter | solution.py:76
  28.7 6.1 %collective-permute-start.8 = (bf16[64,512]{1,0:T(8,128)(2,1)S(1)}, bf16[64,512]{1,0:T(8,128)(2,1)S(1)}, u32[]{:S(2)}, u32[]{:S(2)}) collective-permute-start(bf16[64,512]{1,0:T(8,128)(2,1)S(1)} %get-tuple-element.21), channel_id=1, source_target_pairs={{0,24},{2,26},{4,28},{6,30},{8,0},{10,2},{12,4},{14,6},{16,8},{18,... | collective-permute-start | bytes 196616 | tf_op jit(solution)/shard_map/ppermute | solution.py:9
  32.4 6.1 %collective-permute-start.6 = (bf16[64,512]{1,0:T(8,128)(2,1)S(1)}, bf16[64,512]{1,0:T(8,128)(2,1)S(1)}, u32[]{:S(2)}, u32[]{:S(2)}) collective-permute-start(bf16[64,512]{1,0:T(8,128)(2,1)S(1)} %get-tuple-element.21), channel_id=1, source_target_pairs={{0,8},{2,10},{4,12},{6,14},{8,16},{10,18},{12,20},{14,22},{16,24},... | collective-permute-start | bytes 196616 | tf_op jit(solution)/shard_map/ppermute | solution.py:9
  39.5 105.8 %all-gather.6.cloned.1.call-start = ((), (), s32[]{:S(2)}) async-start(), calls=%async_computation.16 | async-start | bytes 3145728 | tf_op jit(solution)/shard_map/all_gather | solution.py:31
  40.2 105.1 %all-gather.8.cloned.1.call-start = ((), (), s32[]{:S(2)}) async-start(), calls=%async_computation.17 | async-start | bytes 3145728 | tf_op jit(solution)/shard_map/all_gather | solution.py:32
  41.4 69.8 %collective-permute-start.1 = (bf16[512,1024]{1,0:T(8,128)(2,1)}, bf16[512,1024]{1,0:T(8,128)(2,1)S(1)}, u32[]{:S(2)}, u32[]{:S(2)}) collective-permute-start(bf16[512,1024]{1,0:T(8,128)(2,1)} %broadcast_in_dim.20), channel_id=1, source_target_pairs={{0,16},{2,18},{4,20},{6,22},{8,24},{10,26},{12,28},{14,30},{16,0},... | collective-permute-start | bytes 3145736 | tf_op jit(solution)/shard_map/ppermute | solution.py:9
  41.4 147.2 %reduce-scatter.9.cloned.1.call-start = ((), (), s32[]{:S(2)}) async-start(), calls=%async_computation.14 | async-start | bytes 393216 | tf_op jit(solution)/shard_map/reduce_scatter | solution.py:76
  42.5 91.2 %collective-permute-start = (bf16[512,1024]{1,0:T(8,128)(2,1)}, bf16[512,1024]{1,0:T(8,128)(2,1)S(1)}, u32[]{:S(2)}, u32[]{:S(2)}) collective-permute-start(bf16[512,1024]{1,0:T(8,128)(2,1)} %select_bitcast_fusion), channel_id=1, source_target_pairs={{0,16},{2,18},{4,20},{6,22},{8,24},{10,26},{12,28},{14,30},{16,0},... | collective-permute-start | bytes 3145736 | tf_op jit(solution)/shard_map/ppermute | solution.py:9
  118.8 20.4 %collective-permute-start.14 = (bf16[64,512]{1,0:T(8,128)(2,1)}, bf16[64,512]{1,0:T(8,128)(2,1)}, u32[]{:S(2)}, u32[]{:S(2)}) collective-permute-start(bf16[64,512]{1,0:T(8,128)(2,1)} %get-tuple-element.17), channel_id=1, source_target_pairs={{0,28},{2,30},{4,0},{6,2},{8,4},{10,6},{12,8},{14,10},{16,12},{18,... | collective-permute-start | bytes 196616 | tf_op jit(solution)/shard_map/ppermute | solution.py:9
  137.0 7.2 %collective-permute-start.12 = (bf16[64,512]{1,0:T(8,128)(2,1)}, bf16[64,512]{1,0:T(8,128)(2,1)S(1)}, u32[]{:S(2)}, u32[]{:S(2)}) collective-permute-start(bf16[64,512]{1,0:T(8,128)(2,1)} %get-tuple-element.17), channel_id=1, source_target_pairs={{0,4},{2,6},{4,8},{6,10},{8,12},{10,14},{12,16},{14,18},{16,20},{1... | collective-permute-start | bytes 196616 | tf_op jit(solution)/shard_map/ppermute | solution.py:9
  145.3 287.2 %reduce-scatter.11.cloned.1.call-start = ((), (), s32[]{:S(2)}) async-start(), calls=%async_computation.15 | async-start | bytes 393216 | tf_op jit(solution)/shard_map/reduce_scatter | solution.py:76
  174.1 28.2 %collective-permute-start.4 = (bf16[512,1024]{1,0:T(8,128)(2,1)}, bf16[512,1024]{1,0:T(8,128)(2,1)}, u32[]{:S(2)}, u32[]{:S(2)}) collective-permute-start(bf16[512,1024]{1,0:T(8,128)(2,1)} %broadcast_select_fusion.8), channel_id=1, source_target_pairs={{0,8},{2,10},{4,12},{6,14},{8,16},{10,18},{12,20},{14,22},{16,24},... | collective-permute-start | bytes 3145736 | tf_op jit(solution)/shard_map/ppermute | solution.py:9
  174.1 49.4 %collective-permute-start.5 = (bf16[512,1024]{1,0:T(8,128)(2,1)}, bf16[512,1024]{1,0:T(8,128)(2,1)}, u32[]{:S(2)}, u32[]{:S(2)}) collective-permute-start(bf16[512,1024]{1,0:T(8,128)(2,1)} %get-tuple-element.37), channel_id=1, source_target_pairs={{0,24},{2,26},{4,28},{6,30},{8,0},{10,2},{12,4},{14,6},{16,8},{18,... | collective-permute-start | bytes 3145736 | tf_op jit(solution)/shard_map/ppermute | solution.py:9
  182.5 64.8 %collective-permute-start.3 = (bf16[512,1024]{1,0:T(8,128)(2,1)}, bf16[512,1024]{1,0:T(8,128)(2,1)}, u32[]{:S(2)}, u32[]{:S(2)}) collective-permute-start(bf16[512,1024]{1,0:T(8,128)(2,1)} %fusion.104), channel_id=1, source_target_pairs={{0,8},{2,10},{4,12},{6,14},{8,16},{10,18},{12,20},{14,22},{16,24},... | collective-permute-start | bytes 3145736 | tf_op jit(solution)/shard_map/ppermute | solution.py:9
  184.8 83.4 %collective-permute-start.7 = (bf16[512,1024]{1,0:T(8,128)(2,1)}, bf16[512,1024]{1,0:T(8,128)(2,1)}, u32[]{:S(2)}, u32[]{:S(2)}) collective-permute-start(bf16[512,1024]{1,0:T(8,128)(2,1)} %fusion.104), channel_id=1, source_target_pairs={{0,24},{2,26},{4,28},{6,30},{8,0},{10,2},{12,4},{14,6},{16,8},{18,... | collective-permute-start | bytes 3145736 | tf_op jit(solution)/shard_map/ppermute | solution.py:9
  190.4 123.4 %collective-permute-start.18 = (bf16[64,512]{1,0:T(8,128)(2,1)S(1)}, bf16[64,512]{1,0:T(8,128)(2,1)S(1)}, u32[]{:S(2)}, u32[]{:S(2)}) collective-permute-start(bf16[64,512]{1,0:T(8,128)(2,1)S(1)} %get-tuple-element.13), channel_id=1, source_target_pairs={{0,2},{2,4},{4,6},{6,8},{8,10},{10,12},{12,14},{14,16},{16,18},{18... | collective-permute-start | bytes 196616 | tf_op jit(solution)/shard_map/ppermute | solution.py:9
  202.3 105.5 %collective-permute-start.20 = (bf16[64,512]{1,0:T(8,128)(2,1)S(1)}, bf16[64,512]{1,0:T(8,128)(2,1)}, u32[]{:S(2)}, u32[]{:S(2)}) collective-permute-start(bf16[64,512]{1,0:T(8,128)(2,1)S(1)} %get-tuple-element.13), channel_id=1, source_target_pairs={{0,30},{2,0},{4,2},{6,4},{8,6},{10,8},{12,10},{14,12},{16,14},{18,... | collective-permute-start | bytes 196616 | tf_op jit(solution)/shard_map/ppermute | solution.py:9
  233.9 34.3 %copy-start.12 = (bf16[512,1024]{1,0:T(8,128)(2,1)S(1)}, bf16[512,1024]{1,0:T(8,128)(2,1)}, u32[]{:S(2)}) copy-start(bf16[512,1024]{1,0:T(8,128)(2,1)} %get-tuple-element.19) | copy-start | bytes 3145732
  233.9 34.3 %copy-start.20 = (bf16[1024,512]{0,1:T(8,128)(2,1)S(1)}, bf16[1024,512]{0,1:T(8,128)(2,1)}, u32[]{:S(2)}) copy-start(bf16[1024,512]{0,1:T(8,128)(2,1)} %copy.85) | copy-start | bytes 3145732
  297.6 68.7 %collective-permute-start.10 = (bf16[512,1024]{1,0:T(8,128)(2,1)}, bf16[512,1024]{1,0:T(8,128)(2,1)}, u32[]{:S(2)}, u32[]{:S(2)}) collective-permute-start(bf16[512,1024]{1,0:T(8,128)(2,1)} %broadcast_select_fusion.12), channel_id=1, source_target_pairs={{0,4},{2,6},{4,8},{6,10},{8,12},{10,14},{12,16},{14,18},{16,20},{1... | collective-permute-start | bytes 3145736 | tf_op jit(solution)/shard_map/ppermute | solution.py:9
  297.6 71.4 %collective-permute-start.11 = (bf16[512,1024]{1,0:T(8,128)(2,1)}, bf16[512,1024]{1,0:T(8,128)(2,1)}, u32[]{:S(2)}, u32[]{:S(2)}) collective-permute-start(bf16[512,1024]{1,0:T(8,128)(2,1)} %get-tuple-element.32), channel_id=1, source_target_pairs={{0,28},{2,30},{4,0},{6,2},{8,4},{10,6},{12,8},{14,10},{16,12},{18,... | collective-permute-start | bytes 3145736 | tf_op jit(solution)/shard_map/ppermute | solution.py:9
  307.8 80.6 %collective-permute-start.9 = (bf16[512,1024]{1,0:T(8,128)(2,1)}, bf16[512,1024]{1,0:T(8,128)(2,1)}, u32[]{:S(2)}, u32[]{:S(2)}) collective-permute-start(bf16[512,1024]{1,0:T(8,128)(2,1)} %fusion.101), channel_id=1, source_target_pairs={{0,4},{2,6},{4,8},{6,10},{8,12},{10,14},{12,16},{14,18},{16,20},{1... | collective-permute-start | bytes 3145736 | tf_op jit(solution)/shard_map/ppermute | solution.py:9
  308.9 81.8 %collective-permute-start.13 = (bf16[512,1024]{1,0:T(8,128)(2,1)}, bf16[512,1024]{1,0:T(8,128)(2,1)}, u32[]{:S(2)}, u32[]{:S(2)}) collective-permute-start(bf16[512,1024]{1,0:T(8,128)(2,1)} %fusion.101), channel_id=1, source_target_pairs={{0,28},{2,30},{4,0},{6,2},{8,4},{10,6},{12,8},{14,10},{16,12},{18,... | collective-permute-start | bytes 3145736 | tf_op jit(solution)/shard_map/ppermute | solution.py:9
  414.5 71.9 %collective-permute-start.16 = (bf16[512,1024]{1,0:T(8,128)(2,1)S(1)}, bf16[512,1024]{1,0:T(8,128)(2,1)}, u32[]{:S(2)}, u32[]{:S(2)}) collective-permute-start(bf16[512,1024]{1,0:T(8,128)(2,1)S(1)} %broadcast_select_fusion.16), channel_id=1, source_target_pairs={{0,2},{2,4},{4,6},{6,8},{8,10},{10,12},{12,14},{14,16},{16,18},{18... | collective-permute-start | bytes 3145736 | tf_op jit(solution)/shard_map/ppermute | solution.py:9
  417.9 68.5 %collective-permute-start.17 = (bf16[512,1024]{1,0:T(8,128)(2,1)}, bf16[512,1024]{1,0:T(8,128)(2,1)}, u32[]{:S(2)}, u32[]{:S(2)}) collective-permute-start(bf16[512,1024]{1,0:T(8,128)(2,1)} %get-tuple-element.27), channel_id=1, source_target_pairs={{0,30},{2,0},{4,2},{6,4},{8,6},{10,8},{12,10},{14,12},{16,14},{18,... | collective-permute-start | bytes 3145736 | tf_op jit(solution)/shard_map/ppermute | solution.py:9
  424.4 83.7 %collective-permute-start.15 = (bf16[512,1024]{1,0:T(8,128)(2,1)}, bf16[512,1024]{1,0:T(8,128)(2,1)}, u32[]{:S(2)}, u32[]{:S(2)}) collective-permute-start(bf16[512,1024]{1,0:T(8,128)(2,1)} %fusion.98), channel_id=1, source_target_pairs={{0,2},{2,4},{4,6},{6,8},{8,10},{10,12},{12,14},{14,16},{16,18},{18... | collective-permute-start | bytes 3145736 | tf_op jit(solution)/shard_map/ppermute | solution.py:9
  428.3 82.5 %collective-permute-start.19 = (bf16[512,1024]{1,0:T(8,128)(2,1)}, bf16[512,1024]{1,0:T(8,128)(2,1)}, u32[]{:S(2)}, u32[]{:S(2)}) collective-permute-start(bf16[512,1024]{1,0:T(8,128)(2,1)} %fusion.98), channel_id=1, source_target_pairs={{0,30},{2,0},{4,2},{6,4},{8,6},{10,8},{12,10},{14,12},{16,14},{18,... | collective-permute-start | bytes 3145736 | tf_op jit(solution)/shard_map/ppermute | solution.py:9
  (39 other events, 290.9 us)
Sparse Core Ops, SparseCore 0:
  19.1 8.6 reduce-scatter.4
  39.6 6.2 reduce-scatter.6
  47.4 11.7 all-gather.5
  60.5 11.7 all-gather.7
  145.4 5.0 reduce-scatter.8
  314.9 4.1 reduce-scatter.10
where the time goes:
time: 560 us; the launch traced here: 551 us
  waiting for transfers between devices  272 us (49%)
  starting transfers between devices  66.5 us (12%)
  local copies, waits for them, and re-layouts  59.6 us (11%)
  matrix products  58.3 us (10%)
  blocking collectives  47 us (8%)
  other arithmetic  31.7 us (6%)
  between operations  15.3 us (3%)
    ppermute x21, waiting for transfers between devices, from_behind(): lax.ppermute(shard, axis, [(i, (i + by) % devices) for i in range(devices)])  265 us
    ppermute x21, starting transfers between devices, from_behind(): lax.ppermute(shard, axis, [(i, (i + by) % devices) for i in range(devices)])  66.2 us
    dot_general x17, matrix products, product(): jnp.dot(left_matrix, right_matrix, preferred_element_type=jnp.float32)  58.3 us
    all_to_all x4, blocking collectives, body(): lax.all_to_all(jnp.stack([fresh_a, fresh_b]), 'tile', split_axis=2, conca...  26.7 us
    another operation x5, local copies, waits for them, and re-layouts, body(): jnp.stack([fresh_a, fresh_b])  20.6 us
    all_to_all x4, blocking collectives, body(): lax.all_to_all(left_right, 'tile', split_axis=1, concat_axis=0, tiled=True)  18.4 us
  transfers between devices with their start and end apart: 27, of which 18 were waited for; matrix products, arithmetic and copies ran while one was open for 21% of the time, Pallas kernels for 0%

commit v1 on v0

v1 whole, which is shorter than its diff:
```python
import jax
import jax.numpy as jnp
from jax import lax
from jax.sharding import PartitionSpec as P


def level_of(block):
    level = 0
    while (block >> level) & 1:
        level += 1
    return level


def dot(left, right, over):
    return lax.dot_general(left, right, ((over[:1], over[1:]), ((), ())), preferred_element_type=jnp.float32)


def body(pivot_inverse, mult_left, mult_right, mult_tip, root_cross, root_tip):
    count = lax.axis_size("tm")
    levels = count.bit_length() - 1
    block = jnp.mod(lax.axis_index("tm") + 5, count)
    half = lax.axis_index("tile")
    rows = pivot_inverse.shape[1]

    def send(shard, pairs):
        return lax.ppermute(shard, "tm", [((s - 5) % count, (t - 5) % count) for s, t in pairs])

    def whole(shard, axis=0):
        return lax.all_gather(shard, "tile", axis=axis, tiled=True)

    low = (block + 1) & -(block + 1)
    right_child = ((((block + 1) // low) >> 1) & 1) == 1
    inverse_rows = pivot_inverse[0]
    full_near = whole(jnp.where(right_child, mult_left[0], mult_right[0]))
    full_far = whole(jnp.where(right_child, mult_right[0], mult_left[0]))
    full_tip = whole(mult_tip[0])
    own_cols = lambda full: lax.dynamic_slice_in_dim(full, half * rows, rows, 1)
    cols_near, cols_far, cols_tip = own_cols(full_near), own_cols(full_far), own_cols(full_tip)
    turn_near, turn_far, turn_tip = cols_near.T, cols_far.T, cols_tip.T
    tip_own = jnp.dot(root_tip, cols_tip, preferred_element_type=jnp.float32)

    is_root = block == count - 1
    diag = jnp.where(is_root, inverse_rows, jnp.zeros_like(inverse_rows))
    tip = jnp.where(is_root, root_cross, jnp.zeros_like(root_cross))
    cross_left = jnp.zeros_like(inverse_rows)
    cross_right = cross_left
    far_ready = None

    def far_of(level):
        distance = 2**level
        pivots = [b for b in range(count) if level_of(b) == level]
        below = [(b - distance, b) for b in pivots if b >= distance and level_of(b - distance) > level + 1]
        above = [(b + distance, b) for b in pivots if level_of(b + distance) > level + 1]
        if not above:
            return None
        got_diag, got_tip = send(diag, above), send(tip, above)
        if below:
            got_diag = jnp.where(right_child, got_diag, send(diag, below))
            got_tip = jnp.where(right_child, got_tip, send(tip, below))
        return whole(got_diag), whole(got_tip, 1)

    for level in reversed(range(levels)):
        distance = 2**level
        pivots = [b for b in range(count) if level_of(b) == level]
        rights = [(b - distance, b) for b in pivots if b >= distance and level_of(b - distance) == level + 1]
        lefts = [(b + distance, b) for b in pivots if level_of(b + distance) == level + 1]
        near_diag, near_tip = send(diag, lefts), send(tip, lefts)
        if rights:
            near_diag = jnp.where(right_child, send(diag, rights), near_diag)
            near_tip = jnp.where(right_child, send(tip, rights), near_tip)
        near_diag, near_tip = whole(near_diag), whole(near_tip, 1)
        far = far_ready
        far_ready = far_of(level - 1) if level >= 1 else None
        part_near = dot(turn_near, near_diag, (1, 1)) + dot(turn_tip, near_tip, (1, 0))
        part_far = None
        part_tip = jnp.dot(near_tip, cols_near, preferred_element_type=jnp.float32) + tip_own
        if far is not None:
            far_diag, far_tip = far
            between = send(cross_left, [p for p in lefts if p[0] != count - 1])
            between = jnp.where(right_child, send(cross_right, rights), between)
            between = whole(between)
            part_near = part_near + dot(turn_far, between, (1, 1))
            part_far = (
                dot(turn_far, far_diag, (1, 1))
                + dot(turn_tip, far_tip, (1, 0))
                + dot(turn_near, between, (1, 0))
            )
            part_tip = part_tip + jnp.dot(far_tip, cols_far, preferred_element_type=jnp.float32)
        fresh_near = (-part_near).astype(jnp.bfloat16)
        fresh_tip = (-part_tip).astype(jnp.bfloat16)
        total = dot(fresh_near, full_near, (1, 0)) + dot(fresh_tip, full_tip, (0, 0))
        if part_far is not None:
            fresh_far = (-part_far).astype(jnp.bfloat16)
            total = total + dot(fresh_far, full_far, (1, 0))
        else:
            fresh_far = jnp.zeros_like(fresh_near)
        if far is not None:
            exists = right_child | (block >= distance)
            fresh_far = jnp.where(exists, fresh_far, jnp.zeros_like(fresh_far))
        fresh_diag = (inverse_rows.astype(jnp.float32) - total).astype(jnp.bfloat16)
        active = jnp.mod(block, 2 ** (level + 1)) == distance - 1
        diag = jnp.where(active, fresh_diag, diag)
        tip = jnp.where(active, fresh_tip, tip)
        cross_left = jnp.where(active, jnp.where(right_child, fresh_near, fresh_far), cross_left)
        cross_right = jnp.where(active, jnp.where(right_child, fresh_far, fresh_near), cross_right)
    crossing = jnp.concatenate([cross_left, cross_right], axis=1)
    return (diag[None], crossing[None], tip[None])


def solution(mesh):
    placed = (
        P("tm", "tile", None),
        P("tm", "tile", None),
        P("tm", "tile", None),
        P("tm", "tile", None),
        P(None, "tile"),
        P(),
    )
    return jax.shard_map(
        body,
        mesh=mesh,
        in_specs=placed,
        out_specs=(P("tm", "tile", None), P("tm", "tile", None), P("tm", None, "tile")),
        check_vma=False,
    )
```

time: 560 us -> 497 us (0.89)
  local copies, waits for them, and re-layouts: 59.6 us -> 7.35 us
  matrix products: 58.3 us -> 95.3 us
  blocking collectives: 47 us -> 16.5 us
  waiting for transfers between devices: 272 us -> 251 us
  starting transfers between devices: 66.5 us -> 85.4 us
  other arithmetic: 31.7 us -> 18.6 us
    all_to_all x8 -> x0, blocking collectives: 45.1 us -> none  [the longest x4 26.7 us: body(): lax.all_to_all(jnp.stack([fresh_a, fresh_b]), 'tile', split_axis=2, conca...]
    ppermute x21 -> x30, waiting for transfers between devices: 265 us -> 222 us  [send(): lax.ppermute(shard, 'tm', [((s - 5) % count, (t - 5) % count) for s, t in...]
    dot_general x17 -> x39, matrix products: 58.3 us -> 95.3 us  [the longest x31 88.1 us: dot(): lax.dot_general(left, right, ((over[:1], over[1:]), ((), ())), preferred_...]
    all_gather x2 -> x12, waiting for transfers between devices: 0.03 us -> 27.8 us  [whole(): return lax.all_gather(shard, 'tile', axis=axis, tiled=True)]
    another operation x5 -> x0, local copies, waits for them, and re-layouts: 20.6 us -> none  [body(): jnp.stack([fresh_a, fresh_b])]
    ppermute x21 -> x30, starting transfers between devices: 66.2 us -> 84.5 us  [send(): lax.ppermute(shard, 'tm', [((s - 5) % count, (t - 5) % count) for s, t in...]
    all_gather x1 -> x8, blocking collectives: 1.9 us -> 16.5 us  [whole(): return lax.all_gather(shard, 'tile', axis=axis, tiled=True)]
    transpose x12 -> x0, local copies, waits for them, and re-layouts: 10.9 us -> none  [the longest x8 8.55 us: body(): operand = jnp.concatenate([jnp.concatenate([left_diag, left_right, left_t...]
  transfers between devices with their start and end apart: 27 -> 42, of which waited for: 18 -> 8; matrix products, arithmetic and copies ran while one was open for 21% -> 20% of each run, Pallas kernels for 0% -> 0%
where the time goes in v1:
time: 497 us; the launch traced here: 490 us
  waiting for transfers between devices  251 us (51%)
  matrix products  95.3 us (19%)
  starting transfers between devices  85.4 us (17%)
  other arithmetic  18.6 us (4%)
  blocking collectives  16.5 us (3%)
  between operations  15.4 us (3%)
  local copies, waits for them, and re-layouts  7.35 us (1%)
    ppermute x30, waiting for transfers between devices, send(): lax.ppermute(shard, 'tm', [((s - 5) % count, (t - 5) % count) for s, t in...  222 us
    dot_general x31, matrix products, dot(): lax.dot_general(left, right, ((over[:1], over[1:]), ((), ())), preferred_...  88.1 us
    ppermute x30, starting transfers between devices, send(): lax.ppermute(shard, 'tm', [((s - 5) % count, (t - 5) % count) for s, t in...  84.5 us
    all_gather x12, waiting for transfers between devices, whole(): return lax.all_gather(shard, 'tile', axis=axis, tiled=True)  27.8 us
    all_gather x8, blocking collectives, whole(): return lax.all_gather(shard, 'tile', axis=axis, tiled=True)  16.5 us
  transfers between devices with their start and end apart: 42, of which 8 were waited for; matrix products, arithmetic and copies ran while one was open for 20% of the time, Pallas kernels for 0%

profile of v1, /device:TPU:0, one launch (start us, length us, event | category | flops | bytes accessed | tf_op | source)
XLA Modules:
  0.0 489.5 jit_solution(3688597968403237340)
XLA Ops:
  7.3 3.1 broadcast_select_fusion.11
  20.9 2.9 all-gather.36.cloned.1.call-done
  23.8 24.9 %all-gather.16.cloned.1.call-done = bf16[1024,1024]{1,0:T(8,128)(2,1)} async-done(((bf16[512,1024]{1,0:T(8,128)(2,1)}), bf16[1024,1024]{1,0:T(8,128)(2,1)}) %all-gather.16.cloned.1.call-update) | async-done | bytes 2097168 | tf_op jit(solution)/shard_map/all_gather | solution.py:29
  48.7 4.2 select_select_fusion.6
  58.3 2.6 fusion.14
  78.5 4.5 fusion.46
  83.1 127.5 %collective-permute-done.18 = bf16[512,1024]{1,0:T(8,128)(2,1)} collective-permute-done((bf16[512,1024]{1,0:T(8,128)(2,1)}, bf16[512,1024]{1,0:T(8,128)(2,1)}, u32[]{:S(2)}, u32[]{:S(2)}) %collective-permute-start.18) | collective-permute-done | bytes 1048608 | tf_op jit(solution)/shard_map/ppermute | solution.py:26
  213.1 5.1 %negate_convert_fusion.4 = bf16[512,1024]{1,0:T(8,128)(2,1)} fusion(f32[512,1024]{1,0:T(8,128)} %fusion.46, f32[512,1024]{1,0:T(8,128)} %fusion.93, bf16[1024,1024]{1,0:T(8,128)(2,1)} %all-gather.20.cloned.1.call-done, bf16[1,1024,1024]{2,1,0:T(8,128)(2,1)S(1)} %copy-done.3, s32[]{:T(128)S(6)} %select_n.260), kind=kOutput, calls=%fused_computation.27 | convolution fusion | flops 1075838976 | bytes 8388612 | tf_op jit(solution)/shard_map/dot_general | solution.py:15
  218.3 3.3 fusion.71
  222.6 4.6 select_select_fusion.4
  230.8 2.6 fusion.6
  233.4 23.0 %collective-permute-done.14 = bf16[512,1024]{1,0:T(8,128)(2,1)S(1)} collective-permute-done((bf16[512,1024]{1,0:T(8,128)(2,1)S(1)}, bf16[512,1024]{1,0:T(8,128)(2,1)S(1)}, u32[]{:S(2)}, u32[]{:S(2)}) %collective-permute-start.14) | collective-permute-done | bytes 1048608 | tf_op jit(solution)/shard_map/ppermute | solution.py:26
  257.6 2.6 fusion.12
  263.2 26.0 %collective-permute-done.10 = bf16[512,1024]{1,0:T(8,128)(2,1)S(1)} collective-permute-done((bf16[512,1024]{1,0:T(8,128)(2,1)S(1)}, bf16[512,1024]{1,0:T(8,128)(2,1)S(1)}, u32[]{:S(2)}, u32[]{:S(2)}) %collective-permute-start.10) | collective-permute-done | bytes 1048608 | tf_op jit(solution)/shard_map/ppermute | solution.py:26
  308.0 4.5 fusion.40
  315.1 5.1 %negate_convert_fusion.2 = bf16[512,1024]{1,0:T(8,128)(2,1)} fusion(f32[512,1024]{1,0:T(8,128)} %fusion.40, f32[512,1024]{1,0:T(8,128)} %fusion.89, bf16[1024,1024]{1,0:T(8,128)(2,1)} %all-gather.26.cloned.1.call-done, bf16[1,1024,1024]{2,1,0:T(8,128)(2,1)S(1)} %copy-done.3, s32[]{:T(128)S(6)} %select_n.260), kind=kOutput, calls=%fused_computation.25 | convolution fusion | flops 1075838976 | bytes 8388612 | tf_op jit(solution)/shard_map/dot_general | solution.py:15
  320.3 3.1 fusion.66
  323.7 4.0 select_select_fusion.2
  327.7 17.7 %collective-permute-start.24 = (bf16[512,1024]{1,0:T(8,128)(2,1)S(1)}, bf16[512,1024]{1,0:T(8,128)(2,1)S(1)}, u32[]{:S(2)}, u32[]{:S(2)}) collective-permute-start(bf16[512,1024]{1,0:T(8,128)(2,1)S(1)} %get-tuple-element.6), channel_id=1, source_target_pairs={{24,26},{0,2},{8,10},{16,18},{25,27},{1,3},{9,11},{17,19}} | collective-permute-start | bytes 3145736 | tf_op jit(solution)/shard_map/ppermute | solution.py:26
  345.4 26.9 %collective-permute-start.25 = (bf16[512,1024]{1,0:T(8,128)(2,1)S(1)}, bf16[512,1024]{1,0:T(8,128)(2,1)S(1)}, u32[]{:S(2)}, u32[]{:S(2)}) collective-permute-start(bf16[512,1024]{1,0:T(8,128)(2,1)S(1)} %get-tuple-element.5), channel_id=1, source_target_pairs={{24,22},{0,30},{8,6},{16,14},{25,23},{1,31},{9,7},{17,15}} | collective-permute-start | bytes 3145736 | tf_op jit(solution)/shard_map/ppermute | solution.py:26
  373.0 2.6 fusion.4
  375.6 18.8 %collective-permute-done.25 = bf16[512,1024]{1,0:T(8,128)(2,1)S(1)} collective-permute-done((bf16[512,1024]{1,0:T(8,128)(2,1)S(1)}, bf16[512,1024]{1,0:T(8,128)(2,1)S(1)}, u32[]{:S(2)}, u32[]{:S(2)}) %collective-permute-start.25) | collective-permute-done | bytes 1048608 | tf_op jit(solution)/shard_map/ppermute | solution.py:26
  395.6 2.6 fusion.10
  402.2 8.4 %collective-permute-start.21 = (bf16[512,1024]{1,0:T(8,128)(2,1)}, bf16[512,1024]{1,0:T(8,128)(2,1)}, u32[]{:S(2)}, u32[]{:S(2)}) collective-permute-start(bf16[512,1024]{1,0:T(8,128)(2,1)} %fusion.19), channel_id=1, source_target_pairs={{24,22},{0,30},{8,6},{16,14},{25,23},{1,31},{9,7},{17,15}} | collective-permute-start | bytes 3145736 | tf_op jit(solution)/shard_map/ppermute | solution.py:26
  422.4 25.2 %collective-permute-done.20 = bf16[512,1024]{1,0:T(8,128)(2,1)} collective-permute-done((bf16[512,1024]{1,0:T(8,128)(2,1)}, bf16[512,1024]{1,0:T(8,128)(2,1)}, u32[]{:S(2)}, u32[]{:S(2)}) %collective-permute-start.20) | collective-permute-done | bytes 1048608 | tf_op jit(solution)/shard_map/ppermute | solution.py:26
  447.6 2.3 broadcast_select_fusion.5
  456.7 4.6 fusion.34
  461.4 4.3 negate_convert_fusion
  466.6 2.6 fusion.8
  469.2 3.1 fusion.61
  472.7 3.5 select_select_fusion.1
  477.8 2.9 fusion.21
  (213 shorter events, 94.9 us)
Async XLA Ops:
  7.2 16.6 %all-gather.36.cloned.1.call-start = ((), (), s32[]{:S(2)}) async-start(), calls=%async_computation.10 | async-start | bytes 3145728 | tf_op jit(solution)/shard_map/all_gather | solution.py:29
  10.4 38.3 %all-gather.16.cloned.1.call-start = ((), (), s32[]{:S(2)}) async-start(), calls=%async_computation | async-start | bytes 3145728 | tf_op jit(solution)/shard_map/all_gather | solution.py:29
  12.3 66.2 %all-gather.38.cloned.1.call-start = ((), (), s32[]{:S(2)}) async-start(), calls=%async_computation.11 | async-start | bytes 3145728 | tf_op jit(solution)/shard_map/all_gather | solution.py:29
  13.0 65.5 %all-gather.22.cloned.1.call-start = ((), (), s32[]{:S(2)}) async-start(), calls=%async_computation.3 | async-start | bytes 3145728 | tf_op jit(solution)/shard_map/all_gather | solution.py:29
  13.1 6.3 %collective-permute-start.9 = (bf16[512,1024]{1,0:T(8,128)(2,1)S(1)}, bf16[512,1024]{1,0:T(8,128)(2,1)S(1)}, u32[]{:S(2)}, u32[]{:S(2)}) collective-permute-start(bf16[512,1024]{1,0:T(8,128)(2,1)S(1)} %select_bitcast_fusion), channel_id=1, source_target_pairs={{20,12},{21,13}} | collective-permute-start | bytes 3145736 | tf_op jit(solution)/shard_map/ppermute | solution.py:26
  20.4 192.7 %all-gather.20.cloned.1.call-start = ((), (), s32[]{:S(2)}) async-start(), calls=%async_computation.2 | async-start | bytes 3145728 | tf_op jit(solution)/shard_map/all_gather | solution.py:29
  55.8 162.5 %all-gather.18.cloned.1.call-start = ((), (), s32[]{:S(2)}) async-start(), calls=%async_computation.1 | async-start | bytes 3145728 | tf_op jit(solution)/shard_map/all_gather | solution.py:29
  64.4 243.6 %all-gather.28.cloned.1.call-start = ((), (), s32[]{:S(2)}) async-start(), calls=%async_computation.6 | async-start | bytes 3145728 | tf_op jit(solution)/shard_map/all_gather | solution.py:29
  68.0 6.1 %collective-permute-start.4 = (bf16[64,512]{1,0:T(8,128)(2,1)}, bf16[64,512]{1,0:T(8,128)(2,1)S(1)}, u32[]{:S(2)}, u32[]{:S(2)}) collective-permute-start(bf16[64,512]{1,0:T(8,128)(2,1)} %get-tuple-element.14), channel_id=1, source_target_pairs={{4,12},{5,13}} | collective-permute-start | bytes 196616 | tf_op jit(solution)/shard_map/ppermute | solution.py:26
  68.7 5.5 %collective-permute-start.5 = (bf16[64,512]{1,0:T(8,128)(2,1)}, bf16[64,512]{1,0:T(8,128)(2,1)S(1)}, u32[]{:S(2)}, u32[]{:S(2)}) collective-permute-start(bf16[64,512]{1,0:T(8,128)(2,1)} %get-tuple-element.14), channel_id=1, source_target_pairs={{4,28},{5,29}} | collective-permute-start | bytes 196616 | tf_op jit(solution)/shard_map/ppermute | solution.py:26
  69.3 141.2 %collective-permute-start.18 = (bf16[512,1024]{1,0:T(8,128)(2,1)}, bf16[512,1024]{1,0:T(8,128)(2,1)}, u32[]{:S(2)}, u32[]{:S(2)}) collective-permute-start(bf16[512,1024]{1,0:T(8,128)(2,1)} %copy-done.8), channel_id=1, source_target_pairs={{4,0},{20,16},{5,1},{21,17}} | collective-permute-start | bytes 3145736 | tf_op jit(solution)/shard_map/ppermute | solution.py:26
  70.6 139.9 %collective-permute-start.19 = (bf16[512,1024]{1,0:T(8,128)(2,1)}, bf16[512,1024]{1,0:T(8,128)(2,1)}, u32[]{:S(2)}, u32[]{:S(2)}) collective-permute-start(bf16[512,1024]{1,0:T(8,128)(2,1)} %copy-done.8), channel_id=1, source_target_pairs={{4,8},{5,9}} | collective-permute-start | bytes 3145736 | tf_op jit(solution)/shard_map/ppermute | solution.py:26
  212.9 102.2 %all-gather.26.cloned.1.call-start = ((), (), s32[]{:S(2)}) async-start(), calls=%async_computation.5 | async-start | bytes 3145728 | tf_op jit(solution)/shard_map/all_gather | solution.py:29
  227.2 29.2 %collective-permute-start.14 = (bf16[512,1024]{1,0:T(8,128)(2,1)S(1)}, bf16[512,1024]{1,0:T(8,128)(2,1)S(1)}, u32[]{:S(2)}, u32[]{:S(2)}) collective-permute-start(bf16[512,1024]{1,0:T(8,128)(2,1)S(1)} %get-tuple-element.8), channel_id=1, source_target_pairs={{28,0},{12,16},{29,1},{13,17}} | collective-permute-start | bytes 3145736 | tf_op jit(solution)/shard_map/ppermute | solution.py:26
  228.8 27.7 %collective-permute-start.15 = (bf16[512,1024]{1,0:T(8,128)(2,1)S(1)}, bf16[512,1024]{1,0:T(8,128)(2,1)S(1)}, u32[]{:S(2)}, u32[]{:S(2)}) collective-permute-start(bf16[512,1024]{1,0:T(8,128)(2,1)S(1)} %get-tuple-element.7), channel_id=1, source_target_pairs={{28,24},{12,8},{29,25},{13,9}} | collective-permute-start | bytes 3145736 | tf_op jit(solution)/shard_map/ppermute | solution.py:26
  257.5 62.7 %all-gather.24.cloned.1.call-start = ((), (), s32[]{:S(2)}) async-start(), calls=%async_computation.4 | async-start | bytes 3145728 | tf_op jit(solution)/shard_map/all_gather | solution.py:29
  261.0 28.2 %collective-permute-start.10 = (bf16[512,1024]{1,0:T(8,128)(2,1)S(1)}, bf16[512,1024]{1,0:T(8,128)(2,1)S(1)}, u32[]{:S(2)}, u32[]{:S(2)}) collective-permute-start(bf16[512,1024]{1,0:T(8,128)(2,1)S(1)} %fusion.20), channel_id=1, source_target_pairs={{28,0},{12,16},{29,1},{13,17}} | collective-permute-start | bytes 3145736 | tf_op jit(solution)/shard_map/ppermute | solution.py:26
  262.4 26.7 %collective-permute-start.11 = (bf16[512,1024]{1,0:T(8,128)(2,1)S(1)}, bf16[512,1024]{1,0:T(8,128)(2,1)S(1)}, u32[]{:S(2)}, u32[]{:S(2)}) collective-permute-start(bf16[512,1024]{1,0:T(8,128)(2,1)S(1)} %fusion.20), channel_id=1, source_target_pairs={{28,24},{12,8},{29,25},{13,9}} | collective-permute-start | bytes 3145736 | tf_op jit(solution)/shard_map/ppermute | solution.py:26
  290.3 166.4 %all-gather.34.cloned.1.call-start = ((), (), s32[]{:S(2)}) async-start(), calls=%async_computation.9 | async-start | bytes 3145728 | tf_op jit(solution)/shard_map/all_gather | solution.py:29
  290.4 6.2 %collective-permute-start.16 = (bf16[64,512]{1,0:T(8,128)(2,1)S(1)}, bf16[64,512]{1,0:T(8,128)(2,1)S(1)}, u32[]{:S(2)}, u32[]{:S(2)}) collective-permute-start(bf16[64,512]{1,0:T(8,128)(2,1)S(1)} %copy-done.25), channel_id=1, source_target_pairs={{4,0},{20,16},{5,1},{21,17}} | collective-permute-start | bytes 196616 | tf_op jit(solution)/shard_map/ppermute | solution.py:26
  292.9 10.7 %collective-permute-start.12 = (bf16[64,512]{1,0:T(8,128)(2,1)}, bf16[64,512]{1,0:T(8,128)(2,1)S(1)}, u32[]{:S(2)}, u32[]{:S(2)}) collective-permute-start(bf16[64,512]{1,0:T(8,128)(2,1)} %get-tuple-element.17), channel_id=1, source_target_pairs={{28,0},{12,16},{29,1},{13,17}} | collective-permute-start | bytes 196616 | tf_op jit(solution)/shard_map/ppermute | solution.py:26
  294.2 9.4 %collective-permute-start.13 = (bf16[64,512]{1,0:T(8,128)(2,1)}, bf16[64,512]{1,0:T(8,128)(2,1)S(1)}, u32[]{:S(2)}, u32[]{:S(2)}) collective-permute-start(bf16[64,512]{1,0:T(8,128)(2,1)} %get-tuple-element.17), channel_id=1, source_target_pairs={{28,24},{12,8},{29,25},{13,9}} | collective-permute-start | bytes 196616 | tf_op jit(solution)/shard_map/ppermute | solution.py:26
  298.5 14.0 %collective-permute-start.28 = (bf16[512,1024]{1,0:T(8,128)(2,1)}, bf16[512,1024]{1,0:T(8,128)(2,1)}, u32[]{:S(2)}, u32[]{:S(2)}) collective-permute-start(bf16[512,1024]{1,0:T(8,128)(2,1)} %copy-done.10), channel_id=1, source_target_pairs={{28,26},{4,2},{12,10},{20,18},{29,27},{5,3},{13,11},{21,19}} | collective-permute-start | bytes 3145736 | tf_op jit(solution)/shard_map/ppermute | solution.py:26
  300.1 12.4 %collective-permute-start.29 = (bf16[512,1024]{1,0:T(8,128)(2,1)}, bf16[512,1024]{1,0:T(8,128)(2,1)}, u32[]{:S(2)}, u32[]{:S(2)}) collective-permute-start(bf16[512,1024]{1,0:T(8,128)(2,1)} %copy-done.10), channel_id=1, source_target_pairs={{28,30},{4,6},{12,14},{29,31},{5,7},{13,15}} | collective-permute-start | bytes 3145736 | tf_op jit(solution)/shard_map/ppermute | solution.py:26
  314.8 146.5 %all-gather.32.cloned.1.call-start = ((), (), s32[]{:S(2)}) async-start(), calls=%async_computation.8 | async-start | bytes 3145728 | tf_op jit(solution)/shard_map/all_gather | solution.py:29
  327.7 47.9 %collective-permute-start.24 = (bf16[512,1024]{1,0:T(8,128)(2,1)S(1)}, bf16[512,1024]{1,0:T(8,128)(2,1)S(1)}, u32[]{:S(2)}, u32[]{:S(2)}) collective-permute-start(bf16[512,1024]{1,0:T(8,128)(2,1)S(1)} %get-tuple-element.6), channel_id=1, source_target_pairs={{24,26},{0,2},{8,10},{16,18},{25,27},{1,3},{9,11},{17,19}} | collective-permute-start | bytes 3145736 | tf_op jit(solution)/shard_map/ppermute | solution.py:26
  345.4 48.9 %collective-permute-start.25 = (bf16[512,1024]{1,0:T(8,128)(2,1)S(1)}, bf16[512,1024]{1,0:T(8,128)(2,1)S(1)}, u32[]{:S(2)}, u32[]{:S(2)}) collective-permute-start(bf16[512,1024]{1,0:T(8,128)(2,1)S(1)} %get-tuple-element.5), channel_id=1, source_target_pairs={{24,22},{0,30},{8,6},{16,14},{25,23},{1,31},{9,7},{17,15}} | collective-permute-start | bytes 3145736 | tf_op jit(solution)/shard_map/ppermute | solution.py:26
  395.5 73.7 %all-gather.30.cloned.1.call-start = ((), (), s32[]{:S(2)}) async-start(), calls=%async_computation.7 | async-start | bytes 3145728 | tf_op jit(solution)/shard_map/all_gather | solution.py:29
  399.9 47.7 %collective-permute-start.20 = (bf16[512,1024]{1,0:T(8,128)(2,1)}, bf16[512,1024]{1,0:T(8,128)(2,1)}, u32[]{:S(2)}, u32[]{:S(2)}) collective-permute-start(bf16[512,1024]{1,0:T(8,128)(2,1)} %fusion.19), channel_id=1, source_target_pairs={{24,26},{0,2},{8,10},{16,18},{25,27},{1,3},{9,11},{17,19}} | collective-permute-start | bytes 3145736 | tf_op jit(solution)/shard_map/ppermute | solution.py:26
  402.2 45.4 %collective-permute-start.21 = (bf16[512,1024]{1,0:T(8,128)(2,1)}, bf16[512,1024]{1,0:T(8,128)(2,1)}, u32[]{:S(2)}, u32[]{:S(2)}) collective-permute-start(bf16[512,1024]{1,0:T(8,128)(2,1)} %fusion.19), channel_id=1, source_target_pairs={{24,22},{0,30},{8,6},{16,14},{25,23},{1,31},{9,7},{17,15}} | collective-permute-start | bytes 3145736 | tf_op jit(solution)/shard_map/ppermute | solution.py:26
  412.5 37.4 %collective-permute-start.22 = (bf16[64,512]{1,0:T(8,128)(2,1)S(1)}, bf16[64,512]{1,0:T(8,128)(2,1)}, u32[]{:S(2)}, u32[]{:S(2)}) collective-permute-start(bf16[64,512]{1,0:T(8,128)(2,1)S(1)} %get-tuple-element.20), channel_id=1, source_target_pairs={{24,26},{0,2},{8,10},{16,18},{25,27},{1,3},{9,11},{17,19}} | collective-permute-start | bytes 196616 | tf_op jit(solution)/shard_map/ppermute | solution.py:26
  414.4 35.5 %collective-permute-start.23 = (bf16[64,512]{1,0:T(8,128)(2,1)S(1)}, bf16[64,512]{1,0:T(8,128)(2,1)}, u32[]{:S(2)}, u32[]{:S(2)}) collective-permute-start(bf16[64,512]{1,0:T(8,128)(2,1)S(1)} %get-tuple-element.20), channel_id=1, source_target_pairs={{24,22},{0,30},{8,6},{16,14},{25,23},{1,31},{9,7},{17,15}} | collective-permute-start | bytes 196616 | tf_op jit(solution)/shard_map/ppermute | solution.py:26
  (52 other events, 435.4 us)
Sparse Core Ops, SparseCore 0:
  10.5 13.2 all-gather.35
  25.9 22.7 all-gather.15
  50.8 11.7 all-gather.37
  64.0 13.4 all-gather.21
  78.9 54.9 all-gather.19
  135.2 50.2 all-gather.17
  213.0 10.0 all-gather.27
  257.7 8.2 all-gather.25
  290.4 8.3 all-gather.23
  314.9 46.4 all-gather.33
  395.6 24.0 all-gather.31
  450.1 8.8 all-gather.29

commit v2 on v1

--- a/solution.py
+++ b/solution.py
@@ -25,6 +25,15 @@
     def send(shard, pairs):
         return lax.ppermute(shard, "tm", [((s - 5) % count, (t - 5) % count) for s, t in pairs])
 
+    def detour(shard, pairs, via):
+        row = lambda b: (b - 5) % count
+        first = [(row(s), via(row(s), row(t))) for s, t in pairs]
+        last = [(f[1], row(t)) for f, (_, t) in zip(first, pairs)]
+        distinct = len({f[1] for f in first}) == len(first)
+        if not distinct or any(a == b for a, b in first + last):
+            return send(shard, pairs)
+        return lax.ppermute(lax.ppermute(shard, "tm", first), "tm", last)
+
     def whole(shard, axis=0):
         return lax.all_gather(shard, "tile", axis=axis, tiled=True)
 
@@ -46,17 +55,23 @@
     cross_right = cross_left
     far_ready = None
 
-    def far_of(level):
+    def far_of(level, diag, tip):
         distance = 2**level
         pivots = [b for b in range(count) if level_of(b) == level]
         below = [(b - distance, b) for b in pivots if b >= distance and level_of(b - distance) > level + 1]
         above = [(b + distance, b) for b in pivots if level_of(b + distance) > level + 1]
         if not above:
             return None
-        got_diag, got_tip = send(diag, above), send(tip, above)
+        got = [send(diag, above), send(tip, above)]
         if below:
-            got_diag = jnp.where(right_child, got_diag, send(diag, below))
-            got_tip = jnp.where(right_child, got_tip, send(tip, below))
+            got += [send(diag, below), send(tip, below)]
+        return tuple(got)
+
+    def far_whole(got):
+        got_diag, got_tip = got[:2]
+        if len(got) == 4:
+            got_diag = jnp.where(right_child, got_diag, got[2])
+            got_tip = jnp.where(right_child, got_tip, got[3])
         return whole(got_diag), whole(got_tip, 1)
 
     for level in reversed(range(levels)):
@@ -64,20 +79,36 @@
         pivots = [b for b in range(count) if level_of(b) == level]
         rights = [(b - distance, b) for b in pivots if b >= distance and level_of(b - distance) == level + 1]
         lefts = [(b + distance, b) for b in pivots if level_of(b + distance) == level + 1]
-        near_diag, near_tip = send(diag, lefts), send(tip, lefts)
+        send_left, send_right = send, send
+        if level == 0:
+            send_left = lambda shard, pairs: detour(shard, pairs, lambda s, t: s ^ 2)
+        if level == 1:
+            send_right = lambda shard, pairs: detour(shard, pairs, lambda s, t: (t & ~3) | (s & 3))
+        near_tip = send(tip, lefts)
         if rights:
-            near_diag = jnp.where(right_child, send(diag, rights), near_diag)
             near_tip = jnp.where(right_child, send(tip, rights), near_tip)
+        near_diag = send_left(diag, lefts)
+        if rights:
+            near_diag = jnp.where(right_child, send_right(diag, rights), near_diag)
+        between = None
+        if rights:
+            crossed = [p for p in lefts if p[0] != count - 1 and p[1] >= distance]
+            between = send_right(cross_right, rights)
+            if crossed:
+                between = jnp.where(right_child, between, send_left(cross_left, crossed))
+        far = far_ready
+        far_ready = None
+        if level >= 1:
+            arrived = near_diag if between is None else (near_diag, between)
+            arrived, late_diag, late_tip = lax.optimization_barrier((arrived, diag, tip))
+            near_diag, between = (arrived, None) if between is None else arrived
+            far_ready = far_of(level - 1, late_diag, late_tip)
         near_diag, near_tip = whole(near_diag), whole(near_tip, 1)
-        far = far_ready
-        far_ready = far_of(level - 1) if level >= 1 else None
         part_near = dot(turn_near, near_diag, (1, 1)) + dot(turn_tip, near_tip, (1, 0))
         part_far = None
         part_tip = jnp.dot(near_tip, cols_near, preferred_element_type=jnp.float32) + tip_own
         if far is not None:
             far_diag, far_tip = far
-            between = send(cross_left, [p for p in lefts if p[0] != count - 1])
-            between = jnp.where(right_child, send(cross_right, rights), between)
             between = whole(between)
             part_near = part_near + dot(turn_far, between, (1, 1))
             part_far = (
@@ -98,6 +129,9 @@
             exists = right_child | (block >= distance)
             fresh_far = jnp.where(exists, fresh_far, jnp.zeros_like(fresh_far))
         fresh_diag = (inverse_rows.astype(jnp.float32) - total).astype(jnp.bfloat16)
+        if far_ready is not None:
+            fresh_diag, far_ready = lax.optimization_barrier((fresh_diag, far_ready))
+            far_ready = far_whole(far_ready)
         active = jnp.mod(block, 2 ** (level + 1)) == distance - 1
         diag = jnp.where(active, fresh_diag, diag)
         tip = jnp.where(active, fresh_tip, tip)

time: 497 us -> 462 us (0.930)
  starting transfers between devices: 85.4 us -> 67.2 us
  waiting for transfers between devices: 251 us -> 235 us
  other arithmetic: 18.6 us -> 26.4 us
    ppermute x30 -> x25, waiting for transfers between devices: 222 us -> 20.7 us  [send(): lax.ppermute(shard, 'tm', [((s - 5) % count, (t - 5) % count) for s, t in...]
    ppermute x0 -> x8, waiting for transfers between devices: none -> 101 us  [detour(): return lax.ppermute(lax.ppermute(shard, 'tm', first), 'tm', last)]
    all_gather x12, waiting for transfers between devices: 27.8 us -> 111 us  [whole(): return lax.all_gather(shard, 'tile', axis=axis, tiled=True)]
    ppermute x30 -> x25, starting transfers between devices: 84.5 us -> 33.9 us  [send(): lax.ppermute(shard, 'tm', [((s - 5) % count, (t - 5) % count) for s, t in...]
    ppermute x0 -> x8, starting transfers between devices: none -> 32.8 us  [detour(): return lax.ppermute(lax.ppermute(shard, 'tm', first), 'tm', last)]
    dot_general x31, matrix products: 88.1 us -> 80 us  [dot(): lax.dot_general(left, right, ((over[:1], over[1:]), ((), ())), preferred_...]
    select_n x10 -> x12, other arithmetic: 12.5 us -> 20 us  [the longest x3 5.77 us: body(): diag = jnp.where(active, fresh_diag, diag)]
  transfers between devices with their start and end apart: 42 -> 45, of which waited for: 8 -> 13; matrix products, arithmetic and copies ran while one was open for 20% -> 22% of each run, Pallas kernels for 0% -> 0%
where the time goes in v2:
time: 462 us; the launch traced here: 456 us
  waiting for transfers between devices  235 us (51%)
  matrix products  91 us (20%)
  starting transfers between devices  67.2 us (15%)
  other arithmetic  26.4 us (6%)
  blocking collectives  15.9 us (3%)
  between operations  15 us (3%)
  local copies, waits for them, and re-layouts  5.86 us (1%)
    all_gather x12, waiting for transfers between devices, whole(): return lax.all_gather(shard, 'tile', axis=axis, tiled=True)  111 us
    ppermute x8, waiting for transfers between devices, detour(): return lax.ppermute(lax.ppermute(shard, 'tm', first), 'tm', last)  101 us
    dot_general x31, matrix products, dot(): lax.dot_general(left, right, ((over[:1], over[1:]), ((), ())), preferred_...  80 us
    ppermute x25, starting transfers between devices, send(): lax.ppermute(shard, 'tm', [((s - 5) % count, (t - 5) % count) for s, t in...  33.9 us
    ppermute x8, starting transfers between devices, detour(): return lax.ppermute(lax.ppermute(shard, 'tm', first), 'tm', last)  32.8 us
    ppermute x25, waiting for transfers between devices, send(): lax.ppermute(shard, 'tm', [((s - 5) % count, (t - 5) % count) for s, t in...  20.7 us
    all_gather x8, blocking collectives, whole(): return lax.all_gather(shard, 'tile', axis=axis, tiled=True)  15.9 us
  transfers between devices with their start and end apart: 45, of which 13 were waited for; matrix products, arithmetic and copies ran while one was open for 22% of the time, Pallas kernels for 0%

profile of v2, /device:TPU:0, one launch (start us, length us, event | category | flops | bytes accessed | tf_op | source)
XLA Modules:
  0.0 456.4 jit_solution(599498122676484575)
XLA Ops:
  7.3 3.2 broadcast_select_fusion.13
  26.1 23.9 %all-gather.16.cloned.1.call-done = bf16[1024,1024]{1,0:T(8,128)(2,1)} async-done(((bf16[512,1024]{1,0:T(8,128)(2,1)}), bf16[1024,1024]{1,0:T(8,128)(2,1)}) %all-gather.16.cloned.1.call-update) | async-done | bytes 2097168 | tf_op jit(solution)/shard_map/all_gather | solution.py:38
  49.9 4.9 %select_select_fusion.6 = (bf16[512,1024]{1,0:T(8,128)(2,1)}, bf16[512,1024]{1,0:T(8,128)(2,1)S(1)}) fusion(pred[]{:T(512)S(6)} %eq.28, pred[]{:T(512)S(6)} %eq.25, f32[512,1024]{1,0:T(8,128)} %fusion.80, bf16[1024,1024]{1,0:T(8,128)(2,1)} %all-gather.16.cloned.1.call-done, bf16[1,1024,1024]{2,1,0:T(8,128)(2,1)} %all-gather.36.cloned.1.call-done, ...), kind=kOutput, calls=%fused_computation.86 | convolution fusion | flops 1076363264 | bytes 7340038 | tf_op jit(solution)/shard_map/dot_general | solution.py:15
  81.9 6.0 %all-gather.22.cloned.1.call-done = bf16[1024,1024]{1,0:T(8,128)(2,1)} async-done(((bf16[512,1024]{1,0:T(8,128)(2,1)}), bf16[1024,1024]{1,0:T(8,128)(2,1)}) %all-gather.22.cloned.1.call-update) | async-done | bytes 2097168 | tf_op jit(solution)/shard_map/all_gather | solution.py:38
  87.9 4.5 fusion.43
  92.4 68.5 %all-gather.18.cloned.1.call-done = bf16[1024,1024]{1,0:T(8,128)(2,1)} async-done(((bf16[512,1024]{1,0:T(8,128)(2,1)}), bf16[1024,1024]{1,0:T(8,128)(2,1)}) %all-gather.18.cloned.1.call-update) | async-done | bytes 2097168 | tf_op jit(solution)/shard_map/all_gather | solution.py:38
  160.9 4.2 fusion.61
  165.1 9.0 %all-gather.20.cloned.1.call-done = bf16[1024,1024]{1,0:T(8,128)(2,1)} async-done(((bf16[512,1024]{1,0:T(8,128)(2,1)}), bf16[1024,1024]{1,0:T(8,128)(2,1)}) %all-gather.20.cloned.1.call-update) | async-done | bytes 2097168 | tf_op jit(solution)/shard_map/all_gather | solution.py:38
  174.1 4.3 negate_convert_fusion.4
  179.7 4.2 select_select_fusion.4
  186.9 12.3 %collective-permute-done.10 = bf16[64,512]{1,0:T(8,128)(2,1)S(1)} collective-permute-done((bf16[64,512]{1,0:T(8,128)(2,1)}, bf16[64,512]{1,0:T(8,128)(2,1)S(1)}, u32[]{:S(2)}, u32[]{:S(2)}) %collective-permute-start.10) | collective-permute-done | bytes 65568 | tf_op jit(solution)/shard_map/ppermute | solution.py:26
  199.3 2.4 broadcast_select_fusion.4
  212.3 45.3 %collective-permute-done.14 = bf16[512,1024]{1,0:T(8,128)(2,1)S(1)} collective-permute-done((bf16[512,1024]{1,0:T(8,128)(2,1)}, bf16[512,1024]{1,0:T(8,128)(2,1)S(1)}, u32[]{:S(2)}, u32[]{:S(2)}) %collective-permute-start.14) | collective-permute-done | bytes 1048608 | tf_op jit(solution)/shard_map/ppermute | solution.py:35
  258.8 21.5 %collective-permute-done.17 = bf16[512,1024]{1,0:T(8,128)(2,1)} collective-permute-done((bf16[512,1024]{1,0:T(8,128)(2,1)}, bf16[512,1024]{1,0:T(8,128)(2,1)}, u32[]{:S(2)}, u32[]{:S(2)}) %collective-permute-start.17) | collective-permute-done | bytes 1048608 | tf_op jit(solution)/shard_map/ppermute | solution.py:35
  284.6 7.1 %collective-permute-done.19 = bf16[64,512]{1,0:T(8,128)(2,1)S(1)} collective-permute-done((bf16[64,512]{1,0:T(8,128)(2,1)}, bf16[64,512]{1,0:T(8,128)(2,1)S(1)}, u32[]{:S(2)}, u32[]{:S(2)}) %collective-permute-start.19) | collective-permute-done | bytes 65568 | tf_op jit(solution)/shard_map/ppermute | solution.py:26
  305.6 4.5 fusion.37
  310.1 3.0 fusion.54
  313.2 2.7 fusion.41
  317.3 3.1 fusion.57
  326.6 18.4 %collective-permute-start.31 = (bf16[512,1024]{1,0:T(8,128)(2,1)}, bf16[512,1024]{1,0:T(8,128)(2,1)}, u32[]{:S(2)}, u32[]{:S(2)}) collective-permute-start(bf16[512,1024]{1,0:T(8,128)(2,1)} %get-tuple-element.53), channel_id=1, source_target_pairs={{0,4},{8,12},{16,20},{1,5},{9,13},{17,21}} | collective-permute-start | bytes 3145736 | tf_op jit(solution)/shard_map/ppermute | solution.py:35
  349.2 17.5 %collective-permute-done.31 = bf16[512,1024]{1,0:T(8,128)(2,1)} collective-permute-done((bf16[512,1024]{1,0:T(8,128)(2,1)}, bf16[512,1024]{1,0:T(8,128)(2,1)}, u32[]{:S(2)}, u32[]{:S(2)}) %collective-permute-start.31) | collective-permute-done | bytes 1048608 | tf_op jit(solution)/shard_map/ppermute | solution.py:35
  369.7 6.1 %collective-permute-start.26 = (bf16[512,1024]{1,0:T(8,128)(2,1)}, bf16[512,1024]{1,0:T(8,128)(2,1)}, u32[]{:S(2)}, u32[]{:S(2)}) collective-permute-start(bf16[512,1024]{1,0:T(8,128)(2,1)} %broadcast_select_fusion.5), channel_id=1, source_target_pairs={{24,28},{0,4},{8,12},{16,20},{25,29},{1,5},{9,13},{17,21}} | collective-permute-start | bytes 3145736 | tf_op jit(solution)/shard_map/ppermute | solution.py:35
  379.2 17.2 %collective-permute-done.26 = bf16[512,1024]{1,0:T(8,128)(2,1)} collective-permute-done((bf16[512,1024]{1,0:T(8,128)(2,1)}, bf16[512,1024]{1,0:T(8,128)(2,1)}, u32[]{:S(2)}, u32[]{:S(2)}) %collective-permute-start.26) | collective-permute-done | bytes 1048608 | tf_op jit(solution)/shard_map/ppermute | solution.py:35
  399.5 4.7 %collective-permute-start.29 = (bf16[64,512]{1,0:T(8,128)(2,1)S(1)}, bf16[64,512]{1,0:T(8,128)(2,1)}, u32[]{:S(2)}, u32[]{:S(2)}) collective-permute-start(bf16[64,512]{1,0:T(8,128)(2,1)S(1)} %copy-done.27), channel_id=1, source_target_pairs={{24,22},{0,30},{8,6},{16,14},{25,23},{1,31},{9,7},{17,15}} | collective-permute-start | bytes 196616 | tf_op jit(solution)/shard_map/ppermute | solution.py:26
  412.2 2.3 broadcast_select_fusion.8
  420.5 4.5 fusion.31
  425.0 4.3 negate_convert_fusion
  430.3 2.6 fusion.8
  432.9 3.7 all-gather.30.cloned.1.call-done
  436.6 3.0 fusion.52
  440.0 3.5 select_select_fusion.1
  445.1 2.9 fusion.19
  (215 shorter events, 116.2 us)
Async XLA Ops:
  7.2 16.7 %all-gather.36.cloned.1.call-start = ((), (), s32[]{:S(2)}) async-start(), calls=%async_computation.10 | async-start | bytes 3145728 | tf_op jit(solution)/shard_map/all_gather | solution.py:38
  10.5 39.5 %all-gather.16.cloned.1.call-start = ((), (), s32[]{:S(2)}) async-start(), calls=%async_computation | async-start | bytes 3145728 | tf_op jit(solution)/shard_map/all_gather | solution.py:38
  13.3 58.3 %all-gather.38.cloned.1.call-start = ((), (), s32[]{:S(2)}) async-start(), calls=%async_computation.11 | async-start | bytes 3145728 | tf_op jit(solution)/shard_map/all_gather | solution.py:38
  14.1 73.8 %all-gather.22.cloned.1.call-start = ((), (), s32[]{:S(2)}) async-start(), calls=%async_computation.3 | async-start | bytes 3145728 | tf_op jit(solution)/shard_map/all_gather | solution.py:38
  20.7 36.9 %collective-permute-start.2 = (bf16[512,1024]{1,0:T(8,128)(2,1)}, bf16[512,1024]{1,0:T(8,128)(2,1)}, u32[]{:S(2)}, u32[]{:S(2)}) collective-permute-start(bf16[512,1024]{1,0:T(8,128)(2,1)} %select_bitcast_fusion), channel_id=1, source_target_pairs={{20,12},{21,13}} | collective-permute-start | bytes 3145736 | tf_op jit(solution)/shard_map/ppermute | solution.py:26
  22.3 35.3 %collective-permute-start.3 = (bf16[64,512]{1,0:T(8,128)(2,1)S(1)}, bf16[64,512]{1,0:T(8,128)(2,1)}, u32[]{:S(2)}, u32[]{:S(2)}) collective-permute-start(bf16[64,512]{1,0:T(8,128)(2,1)S(1)} %broadcast_select_fusion.23), channel_id=1, source_target_pairs={{20,12},{21,13}} | collective-permute-start | bytes 196616 | tf_op jit(solution)/shard_map/ppermute | solution.py:26
  57.6 103.3 %all-gather.18.cloned.1.call-start = ((), (), s32[]{:S(2)}) async-start(), calls=%async_computation.1 | async-start | bytes 3145728 | tf_op jit(solution)/shard_map/all_gather | solution.py:38
  62.9 111.2 %all-gather.20.cloned.1.call-start = ((), (), s32[]{:S(2)}) async-start(), calls=%async_computation.2 | async-start | bytes 3145728 | tf_op jit(solution)/shard_map/all_gather | solution.py:38
  63.5 242.0 %all-gather.28.cloned.1.call-start = ((), (), s32[]{:S(2)}) async-start(), calls=%async_computation.6 | async-start | bytes 3145728 | tf_op jit(solution)/shard_map/all_gather | solution.py:38
  76.8 122.4 %collective-permute-start.9 = (bf16[512,1024]{1,0:T(8,128)(2,1)}, bf16[512,1024]{1,0:T(8,128)(2,1)}, u32[]{:S(2)}, u32[]{:S(2)}) collective-permute-start(bf16[512,1024]{1,0:T(8,128)(2,1)} %broadcast_select_fusion.3), channel_id=1, source_target_pairs={{4,0},{20,16},{5,1},{21,17}} | collective-permute-start | bytes 3145736 | tf_op jit(solution)/shard_map/ppermute | solution.py:26
  78.1 121.2 %collective-permute-start.11 = (bf16[512,1024]{1,0:T(8,128)(2,1)}, bf16[512,1024]{1,0:T(8,128)(2,1)}, u32[]{:S(2)}, u32[]{:S(2)}) collective-permute-start(bf16[512,1024]{1,0:T(8,128)(2,1)} %broadcast_select_fusion.3), channel_id=1, source_target_pairs={{4,8},{5,9}} | collective-permute-start | bytes 3145736 | tf_op jit(solution)/shard_map/ppermute | solution.py:26
  79.8 119.5 %collective-permute-start.10 = (bf16[64,512]{1,0:T(8,128)(2,1)}, bf16[64,512]{1,0:T(8,128)(2,1)S(1)}, u32[]{:S(2)}, u32[]{:S(2)}) collective-permute-start(bf16[64,512]{1,0:T(8,128)(2,1)} %get-tuple-element.36), channel_id=1, source_target_pairs={{4,0},{20,16},{5,1},{21,17}} | collective-permute-start | bytes 196616 | tf_op jit(solution)/shard_map/ppermute | solution.py:26
  81.1 118.2 %collective-permute-start.12 = (bf16[64,512]{1,0:T(8,128)(2,1)}, bf16[64,512]{1,0:T(8,128)(2,1)S(1)}, u32[]{:S(2)}, u32[]{:S(2)}) collective-permute-start(bf16[64,512]{1,0:T(8,128)(2,1)} %get-tuple-element.36), channel_id=1, source_target_pairs={{4,8},{5,9}} | collective-permute-start | bytes 196616 | tf_op jit(solution)/shard_map/ppermute | solution.py:26
  207.3 102.8 %all-gather.26.cloned.1.call-start = ((), (), s32[]{:S(2)}) async-start(), calls=%async_computation.5 | async-start | bytes 3145728 | tf_op jit(solution)/shard_map/all_gather | solution.py:38
  208.1 49.6 %collective-permute-start.14 = (bf16[512,1024]{1,0:T(8,128)(2,1)}, bf16[512,1024]{1,0:T(8,128)(2,1)S(1)}, u32[]{:S(2)}, u32[]{:S(2)}) collective-permute-start(bf16[512,1024]{1,0:T(8,128)(2,1)} %collective-permute-done.13), channel_id=1, source_target_pairs={{4,0},{20,16},{5,1},{21,17}} | collective-permute-start | bytes 3145736 | tf_op jit(solution)/shard_map/ppermute | solution.py:35
  209.4 49.4 %collective-permute-start.18 = (bf16[512,1024]{1,0:T(8,128)(2,1)}, bf16[512,1024]{1,0:T(8,128)(2,1)}, u32[]{:S(2)}, u32[]{:S(2)}) collective-permute-start(bf16[512,1024]{1,0:T(8,128)(2,1)} %get-tuple-element.55), channel_id=1, source_target_pairs={{12,8},{13,9}} | collective-permute-start | bytes 3145736 | tf_op jit(solution)/shard_map/ppermute | solution.py:26
  211.0 69.2 %collective-permute-start.17 = (bf16[512,1024]{1,0:T(8,128)(2,1)}, bf16[512,1024]{1,0:T(8,128)(2,1)}, u32[]{:S(2)}, u32[]{:S(2)}) collective-permute-start(bf16[512,1024]{1,0:T(8,128)(2,1)} %collective-permute-done.16), channel_id=1, source_target_pairs={{4,0},{20,16},{5,1},{21,17}} | collective-permute-start | bytes 3145736 | tf_op jit(solution)/shard_map/ppermute | solution.py:35
  282.6 34.7 %all-gather.24.cloned.1.call-start = ((), (), s32[]{:S(2)}) async-start(), calls=%async_computation.4 | async-start | bytes 3145728 | tf_op jit(solution)/shard_map/all_gather | solution.py:38
  282.6 9.1 %collective-permute-start.19 = (bf16[64,512]{1,0:T(8,128)(2,1)}, bf16[64,512]{1,0:T(8,128)(2,1)S(1)}, u32[]{:S(2)}, u32[]{:S(2)}) collective-permute-start(bf16[64,512]{1,0:T(8,128)(2,1)} %get-tuple-element.45), channel_id=1, source_target_pairs={{28,0},{12,16},{29,1},{13,17}} | collective-permute-start | bytes 196616 | tf_op jit(solution)/shard_map/ppermute | solution.py:26
  293.6 126.8 %all-gather.34.cloned.1.call-start = ((), (), s32[]{:S(2)}) async-start(), calls=%async_computation.9 | async-start | bytes 3145728 | tf_op jit(solution)/shard_map/all_gather | solution.py:38
  299.7 26.9 %collective-permute-start.21 = (bf16[512,1024]{1,0:T(8,128)(2,1)}, bf16[512,1024]{1,0:T(8,128)(2,1)}, u32[]{:S(2)}, u32[]{:S(2)}) collective-permute-start(bf16[512,1024]{1,0:T(8,128)(2,1)} %broadcast_select_fusion.4), channel_id=1, source_target_pairs={{28,26},{4,2},{12,10},{20,18},{29,27},{5,3},{13,11},{21,19}} | collective-permute-start | bytes 3145736 | tf_op jit(solution)/shard_map/ppermute | solution.py:26
  301.4 25.2 %collective-permute-start.23 = (bf16[512,1024]{1,0:T(8,128)(2,1)}, bf16[512,1024]{1,0:T(8,128)(2,1)}, u32[]{:S(2)}, u32[]{:S(2)}) collective-permute-start(bf16[512,1024]{1,0:T(8,128)(2,1)} %broadcast_select_fusion.4), channel_id=1, source_target_pairs={{28,30},{4,6},{12,14},{29,31},{5,7},{13,15}} | collective-permute-start | bytes 3145736 | tf_op jit(solution)/shard_map/ppermute | solution.py:26
  303.0 23.6 %collective-permute-start.22 = (bf16[64,512]{1,0:T(8,128)(2,1)}, bf16[64,512]{1,0:T(8,128)(2,1)}, u32[]{:S(2)}, u32[]{:S(2)}) collective-permute-start(bf16[64,512]{1,0:T(8,128)(2,1)} %get-tuple-element.45), channel_id=1, source_target_pairs={{28,26},{4,2},{12,10},{20,18},{29,27},{5,3},{13,11},{21,19}} | collective-permute-start | bytes 196616 | tf_op jit(solution)/shard_map/ppermute | solution.py:26
  304.3 22.3 %collective-permute-start.24 = (bf16[64,512]{1,0:T(8,128)(2,1)}, bf16[64,512]{1,0:T(8,128)(2,1)}, u32[]{:S(2)}, u32[]{:S(2)}) collective-permute-start(bf16[64,512]{1,0:T(8,128)(2,1)} %get-tuple-element.45), channel_id=1, source_target_pairs={{28,30},{4,6},{12,14},{29,31},{5,7},{13,15}} | collective-permute-start | bytes 196616 | tf_op jit(solution)/shard_map/ppermute | solution.py:26
  326.6 40.0 %collective-permute-start.31 = (bf16[512,1024]{1,0:T(8,128)(2,1)}, bf16[512,1024]{1,0:T(8,128)(2,1)}, u32[]{:S(2)}, u32[]{:S(2)}) collective-permute-start(bf16[512,1024]{1,0:T(8,128)(2,1)} %get-tuple-element.53), channel_id=1, source_target_pairs={{0,4},{8,12},{16,20},{1,5},{9,13},{17,21}} | collective-permute-start | bytes 3145736 | tf_op jit(solution)/shard_map/ppermute | solution.py:35
  347.4 77.6 %all-gather.32.cloned.1.call-start = ((), (), s32[]{:S(2)}) async-start(), calls=%async_computation.8 | async-start | bytes 3145728 | tf_op jit(solution)/shard_map/all_gather | solution.py:38
  347.5 28.3 %collective-permute-start.30 = (bf16[512,1024]{1,0:T(8,128)(2,1)}, bf16[512,1024]{1,0:T(8,128)(2,1)S(1)}, u32[]{:S(2)}, u32[]{:S(2)}) collective-permute-start(bf16[512,1024]{1,0:T(8,128)(2,1)} %get-tuple-element.54), channel_id=1, source_target_pairs={{24,26},{0,2},{8,10},{16,18},{25,27},{1,3},{9,11},{17,19}} | collective-permute-start | bytes 3145736 | tf_op jit(solution)/shard_map/ppermute | solution.py:26
  366.7 9.1 %collective-permute-start.32 = (bf16[512,1024]{1,0:T(8,128)(2,1)}, bf16[512,1024]{1,0:T(8,128)(2,1)S(1)}, u32[]{:S(2)}, u32[]{:S(2)}) collective-permute-start(bf16[512,1024]{1,0:T(8,128)(2,1)} %collective-permute-done.31), channel_id=1, source_target_pairs={{4,30},{12,6},{20,14},{5,31},{13,7},{21,15}} | collective-permute-start | bytes 3145736 | tf_op jit(solution)/shard_map/ppermute | solution.py:35
  369.7 26.8 %collective-permute-start.26 = (bf16[512,1024]{1,0:T(8,128)(2,1)}, bf16[512,1024]{1,0:T(8,128)(2,1)}, u32[]{:S(2)}, u32[]{:S(2)}) collective-permute-start(bf16[512,1024]{1,0:T(8,128)(2,1)} %broadcast_select_fusion.5), channel_id=1, source_target_pairs={{24,28},{0,4},{8,12},{16,20},{25,29},{1,5},{9,13},{17,21}} | collective-permute-start | bytes 3145736 | tf_op jit(solution)/shard_map/ppermute | solution.py:35
  376.9 59.6 %all-gather.30.cloned.1.call-start = ((), (), s32[]{:S(2)}) async-start(), calls=%async_computation.7 | async-start | bytes 3145728 | tf_op jit(solution)/shard_map/all_gather | solution.py:38
  377.0 35.2 %collective-permute-start.25 = (bf16[512,1024]{1,0:T(8,128)(2,1)}, bf16[512,1024]{1,0:T(8,128)(2,1)}, u32[]{:S(2)}, u32[]{:S(2)}) collective-permute-start(bf16[512,1024]{1,0:T(8,128)(2,1)} %broadcast_select_fusion.5), channel_id=1, source_target_pairs={{24,26},{0,2},{8,10},{16,18},{25,27},{1,3},{9,11},{17,19}} | collective-permute-start | bytes 3145736 | tf_op jit(solution)/shard_map/ppermute | solution.py:26
  396.5 15.8 %collective-permute-start.27 = (bf16[512,1024]{1,0:T(8,128)(2,1)}, bf16[512,1024]{1,0:T(8,128)(2,1)}, u32[]{:S(2)}, u32[]{:S(2)}) collective-permute-start(bf16[512,1024]{1,0:T(8,128)(2,1)} %collective-permute-done.26), channel_id=1, source_target_pairs={{28,22},{4,30},{12,6},{20,14},{29,23},{5,31},{13,7},{21,15}} | collective-permute-start | bytes 3145736 | tf_op jit(solution)/shard_map/ppermute | solution.py:35
  (52 other events, 227.7 us)
Sparse Core Ops, SparseCore 0:
  10.6 13.2 all-gather.35
  25.4 24.4 all-gather.15
  51.5 11.7 all-gather.37
  64.7 23.2 all-gather.21
  89.3 71.5 all-gather.17
  162.3 11.7 all-gather.19
  207.4 14.0 all-gather.27
  282.7 6.4 all-gather.25
  293.8 8.7 all-gather.23
  347.5 16.1 all-gather.33
  377.0 27.3 all-gather.31
  414.7 21.8 all-gather.29
